TPU v7x, 32 devices: a whole 2x2x4 slice. The times are simulated.
32 devices in a mesh: ctx: 8 (over z, y), head: 4 (over x, core).
Axes of the slice: x: 2, y: 2, z: 4, core: 2. Of those that a mesh axis runs over, the one named last changes fastest.
Arguments:
- query_self: bfloat16 [512, 8192], P('ctx', 'head'), may hold values from -60 to 60
- key_self: bfloat16 [512, 1024], P('ctx', 'head'), may hold values from -6 to 6
- value_self: bfloat16 [512, 1024], P('ctx', 'head'), may hold values from -6 to 6
- positions: int32 [512], P('ctx'), may hold values from 0 to 1533, as said below
- query_cross: bfloat16 [512, 8192], P('ctx', 'head'), may hold values from -60 to 60
- key_vision: bfloat16 [7168, 1024], P('ctx', 'head'), may hold values from -6 to 6
- value_vision: bfloat16 [7168, 1024], P('ctx', 'head'), may hold values from -6 to 6
- media_range: int32 [32, 2], P('ctx'), may hold values from 0 to 8, as said below
- gate_scale: float32 [1], replicated, may hold values from 0.3 to 1.5
Outputs:
- self_context: bfloat16 [512, 8192], P(('ctx', 'head'))
- cross_context: bfloat16 [512, 8192], P(('ctx', 'head'))
Inputs may be any that keep to these rules, and one draw needn't show every extreme that they name: `positions`: strictly increasing along the transcript, starting at 0; gaps of 1 to 3 up to the next-to-last token, and the last token's position is exactly 1533. `media_range`: column 0 never exceeds column 1; column 1 never falls from block to block, is 0 for the leading blocks (which see no frame) and 8 for the last block.
All inputs are finite; a program needn't handle non-finite values.
Results may differ from a plain program's by a relative error of at most 0.0091.
Values may be sent and summed in bfloat16 or wider, within the bound.
No kernel may reach another device: no remote copies, remote signals or barrier semaphores. Data moves between devices by JAX's collectives and lax.ppermute only.
A program may use at most 64 MiB of HBM per device.

v0:
```python
import functools

import jax
import jax.numpy as jnp
import numpy as np
from jax import lax
from jax.experimental import pallas as pl
from jax.experimental.pallas import tpu as pltpu
from jax.sharding import PartitionSpec as P

HD = 128
TBLOCK = 16
FRAME_LEN = 896


rope_base = 500000.0
lowest = -1e30


def rotate(values, positions):
    half_width = values.shape[-1] // 2
    exponents = jnp.arange(half_width, dtype=jnp.float32) * (2.0 / values.shape[-1])
    frequency = jnp.power(rope_base, -exponents)
    angles = positions.astype(jnp.float32)[:, None] * frequency[None, :]
    cosine = jnp.cos(angles)[:, None, :]
    sine_part = jnp.sin(angles)[:, None, :]
    first_half = values[..., :half_width]
    second_half = values[..., half_width:]
    return jnp.concatenate(
        [
            first_half * cosine - second_half * sine_part,
            second_half * cosine + first_half * sine_part,
        ],
        axis=-1,
    )


def key_block(key_count):
    block_size = min(key_count, 1024)
    while key_count % block_size != 0:
        block_size = block_size - 1
    return block_size


def attend_block(state_in, queries, key_rows, value_rows, allowed):
    maxima, totals, accumulated = state_in
    scale_factor = queries.shape[-1] ** (-0.5)
    scores = (
        jnp.einsum("rkgd,nkd->kgrn", queries, key_rows, preferred_element_type=jnp.float32)
        * scale_factor
    )
    visible = allowed[None, None, :, :]
    scores = jnp.where(visible, scores, lowest)
    new_maxima = jnp.maximum(maxima, jnp.max(scores, axis=-1))
    weights = jnp.where(visible, jnp.exp(scores - new_maxima[..., None]), 0.0)
    factor = jnp.exp(maxima - new_maxima)
    totals = totals * factor + jnp.sum(weights, axis=-1)
    accumulated = accumulated * factor[..., None] + jnp.einsum(
        "kgrn,nkd->kgrd",
        weights.astype(jnp.bfloat16),
        value_rows,
        preferred_element_type=jnp.float32,
    )
    return (new_maxima, totals, accumulated)


def attend(state_in, queries, key_rows, value_rows, allowed):
    key_count = key_rows.shape[0]
    block_size = key_block(key_count)
    if block_size == key_count:
        return attend_block(state_in, queries, key_rows, value_rows, allowed)

    def step_block(block_index, state_now):
        row_begin = block_index * block_size
        key_part = lax.dynamic_slice_in_dim(key_rows, row_begin, block_size, 0)
        value_part = lax.dynamic_slice_in_dim(value_rows, row_begin, block_size, 0)
        allowed_part = lax.dynamic_slice_in_dim(allowed, row_begin, block_size, 1)
        return attend_block(state_now, queries, key_part, value_part, allowed_part)

    return lax.fori_loop(0, key_count // block_size, step_block, state_in)


def keep_state(current):
    return current


def empty_state(row_count, kv_heads, group_size, head_size):
    maxima = jnp.full((kv_heads, group_size, row_count), lowest, jnp.float32)
    totals = jnp.zeros((kv_heads, group_size, row_count), jnp.float32)
    accumulated = jnp.zeros((kv_heads, group_size, row_count, head_size), jnp.float32)
    return (maxima, totals, accumulated)


def finish(state_in):
    maxima, totals, accumulated = state_in
    safe_totals = jnp.where(totals > 0.0, totals, 1.0)
    result = accumulated / safe_totals[..., None]
    kv_heads, group_size, row_count, head_size = result.shape
    return jnp.transpose(result, (2, 0, 1, 3)).reshape(row_count, kv_heads * group_size * head_size)


def causal_group(current, group, key_rows, value_rows, key_index, offset):
    queries, row_index = group
    allowed = key_index[None, :] <= row_index[:, None]

    def causal_compute(state_in):
        return attend(state_in, queries, key_rows, value_rows, allowed)

    return lax.cond(offset <= jnp.max(row_index), causal_compute, keep_state, current)


def frame_mask(frame_index, lower_frame, upper_frame):
    return jnp.logical_and(
        frame_index[None, :] >= lower_frame[:, None], frame_index[None, :] < upper_frame[:, None]
    )


def on_device_gathered(
    query_self,
    key_self,
    value_self,
    positions,
    query_cross,
    key_vision,
    value_vision,
    media_range,
    gate_scale,
):
    head_size = HD
    kv_heads = key_self.shape[1] // head_size
    group_size = query_self.shape[1] // key_self.shape[1]
    row_count = query_self.shape[0]
    vision_count = key_vision.shape[0]
    device = lax.axis_index("ctx")
    own_rows = device * row_count + jnp.arange(row_count, dtype=jnp.int32)
    rotated_query = rotate(
        query_self.astype(jnp.float32).reshape(row_count, kv_heads * group_size, head_size),
        positions,
    )
    rotated_query = rotated_query.astype(jnp.bfloat16).reshape(
        row_count, kv_heads, group_size, head_size
    )
    rotated_key = rotate(
        key_self.astype(jnp.float32).reshape(row_count, kv_heads, head_size), positions
    ).astype(jnp.bfloat16)
    self_values = value_self.reshape(row_count, kv_heads, head_size)
    vision_keys = key_vision.reshape(vision_count, kv_heads, head_size)
    vision_values = value_vision.reshape(vision_count, kv_heads, head_size)
    cross_queries = query_cross.reshape(row_count, kv_heads, group_size, head_size)
    lower_frame = jnp.repeat(media_range[:, 0], TBLOCK)
    upper_frame = jnp.repeat(media_range[:, 1], TBLOCK)
    has_frames = upper_frame > lower_frame
    query_groups = ((rotated_query, own_rows),)
    self_start = tuple(
        (empty_state(group[1].shape[0], kv_heads, group_size, head_size) for group in query_groups)
    )
    cross_start = empty_state(row_count, kv_heads, group_size, head_size)
    offset = jnp.int32(0)
    key_rows = lax.all_gather(rotated_key, "ctx", axis=0, tiled=True)
    value_rows = lax.all_gather(self_values, "ctx", axis=0, tiled=True)
    key_index = jnp.arange(key_rows.shape[0], dtype=jnp.int32)
    updated = []
    for current, group in zip(self_start, query_groups):
        updated.append(causal_group(current, group, key_rows, value_rows, key_index, offset))
    self_states = tuple(updated)
    key_rows = lax.all_gather(vision_keys, "ctx", axis=0, tiled=True)
    value_rows = lax.all_gather(vision_values, "ctx", axis=0, tiled=True)
    frame_index = jnp.arange(key_rows.shape[0], dtype=jnp.int32) // FRAME_LEN
    allowed = frame_mask(frame_index, lower_frame, upper_frame)
    touching = jnp.logical_and(lower_frame <= frame_index[-1], upper_frame > frame_index[0])
    needed = jnp.any(jnp.logical_and(has_frames, touching))

    def fold_compute(state_in):
        return attend(state_in, cross_queries, key_rows, value_rows, allowed)

    cross_state = lax.cond(needed, fold_compute, keep_state, cross_start)
    self_rows = finish(self_states[0]).astype(jnp.bfloat16)
    cross_rows = jnp.where(
        has_frames[:, None], jnp.tanh(gate_scale[0]) * finish(cross_state), 0.0
    ).astype(jnp.bfloat16)
    self_context, cross_context = (
        lax.all_to_all(self_rows, "head", split_axis=0, concat_axis=1, tiled=True),
        lax.all_to_all(cross_rows, "head", split_axis=0, concat_axis=1, tiled=True),
    )
    return (self_context, cross_context)


log2e = 1.4426950408889634
stat_rows = 16
score_limit = 100.0
unseen = -1e30
contract_last = (((1,), (1,)), ((), ()))


def whole(count):
    return [pl.BlockSpec(memory_space=pltpu.VMEM)] * count


def largest_square(values):
    sums = lax.dot_general(
        jnp.ones((8, values.shape[1]), jnp.bfloat16),
        values * values,
        contract_last,
        preferred_element_type=jnp.float32,
    )
    return jnp.max(jnp.max(sums, axis=0, keepdims=True), axis=1, keepdims=True)


def prepare_kernel(
    inner,
    first,
    range_ref,
    position_ref,
    frequency_ref,
    vision_key_ref,
    vision_value_ref,
    cross_ref,
    query_ref,
    key_ref,
    value_ref,
    *refs,
):
    if first:
        vision_out, packet_out = refs[:2]
    else:
        vision_out, packet_out, self_out, across_out = refs[:4]
    range_table, position_row, frequency_row, vision_rows, cross_rows = refs[-13:-8]
    query_rows, key_rows = refs[-8:-6]
    value_rows, packet_rows, self_rows, pair_rows, in_semaphores, out_semaphores = refs[-6:]
    rows, group = cross_rows.shape
    heads = group // HD
    vision = vision_key_ref.shape[0]
    stacked = heads * rows
    place = lax.rem(lax.axis_index("ctx"), inner)
    sides = (place, 1 - place)
    vision_side, packet_side = (sides[0], sides[1]) if first else (sides[1], sides[0])

    def head_columns(head):
        return pl.ds(pl.multiple_of(head * HD, HD), HD)

    def load(source, target):
        copy = pltpu.make_async_copy(source, target, in_semaphores.at[len(loads)])
        copy.start()
        loads.append(copy)

    def store(source, target):
        copy = pltpu.make_async_copy(source, target, out_semaphores.at[len(stores)])
        copy.start()
        stores.append(copy)

    loads, stores = [], []
    load(position_ref, position_row)
    load(frequency_ref, frequency_row)
    load(range_ref, range_table)
    load(cross_ref.at[:, pl.ds(pl.multiple_of(packet_side * group, group), group)], cross_rows)
    load(key_ref, key_rows)
    load(value_ref, value_rows)
    for slot, source in enumerate((vision_key_ref, vision_value_ref)):
        load(
            source.at[:, head_columns(vision_side)], vision_rows.at[pl.ds(slot * vision, vision), :]
        )
    if not first:
        load(query_ref, query_rows)

    def stack(target, head, block):
        for step in range(rows // TBLOCK):
            row = (step * heads + head) * TBLOCK
            target[row : row + TBLOCK, :] = block[step * TBLOCK : (step + 1) * TBLOCK]

    for copy in loads[:2]:
        copy.wait()
    place_of_row = jnp.broadcast_to(position_row[...].astype(jnp.float32), (HD, rows)).T
    frequency = jnp.concatenate([frequency_row[...]] * 2, axis=1)
    angles = place_of_row * frequency
    cosine = jnp.cos(angles)
    column = lax.broadcasted_iota(jnp.int32, angles.shape, 1)
    sine = jnp.sin(angles) * jnp.where(column < HD // 2, -1.0, 1.0)

    def turned(block):
        block = block.astype(jnp.float32)
        return (block * cosine + pltpu.roll(block, HD // 2, 1) * sine).astype(jnp.bfloat16)

    for copy in loads[2:6]:
        copy.wait()
    lane = lax.broadcasted_iota(jnp.int32, (TBLOCK, HD), 1)
    ranges = jnp.zeros((TBLOCK, HD), jnp.int32)
    for item in range(2 * rows // TBLOCK):
        ranges = jnp.where(lane == item, range_table[item % 2, item // 2], ranges)
    ranges = ranges.astype(jnp.float32)
    for head in range(heads):
        stack(packet_rows, head, cross_rows[:, head * HD : (head + 1) * HD])
    packet_rows[stacked : stacked + rows, :] = turned(key_rows[:, head_columns(packet_side)])
    packet_rows[stacked + rows : stacked + 2 * rows, :] = value_rows[:, head_columns(packet_side)]
    largest = largest_square(packet_rows[:stacked, :]) * 1.02 + 2.0
    ranges = jnp.where(lane == 2 * rows // TBLOCK, largest, ranges).astype(jnp.bfloat16)
    packet_rows[stacked + 2 * rows :, :] = ranges
    store(packet_rows, packet_out)
    with_self = vision_out if first else across_out
    pair_rows[:rows, :] = turned(key_rows[:, head_columns(vision_side)])
    pair_rows[rows:, :] = value_rows[:, head_columns(vision_side)]
    store(pair_rows, with_self.at[pl.ds(2 * vision, 2 * rows), :])
    for slot, copy in enumerate(loads[6:8]):
        span = pl.ds(slot * vision, vision)
        copy.wait()
        store(vision_rows.at[span, :], vision_out.at[span, :])
        if not first:
            store(vision_rows.at[span, :], across_out.at[span, :])
    if not first:
        loads[8].wait()
        tails = (vision_out.at[pl.ds(2 * vision, stacked), :], self_out)
        for side, target in zip((1, 0), tails):
            part = self_rows.at[pl.ds(side * stacked, stacked), :]
            for head in range(heads):
                stack(part, head, turned(query_rows[:, head_columns(sides[side] * heads + head)]))
            store(part, target)
    for copy in stores:
        copy.wait()


def prepare(ranges, positions, frequency, vision_keys, vision_values, cross, query, key, value, inner, first):
    rows, columns = query.shape
    group = columns // inner
    stacked = rows * (group // HD)
    vision = vision_keys.shape[0]
    packet = stacked + 2 * rows + TBLOCK
    counts = [2 * vision + 2 * rows, packet]
    if not first:
        counts = [2 * vision + stacked, packet, stacked, 2 * vision + 2 * rows]
    return pl.pallas_call(
        functools.partial(prepare_kernel, inner, first),
        out_shape=[jax.ShapeDtypeStruct((count, HD), jnp.bfloat16) for count in counts],
        in_specs=[pl.BlockSpec(memory_space=pl.ANY)] * 9,
        out_specs=[pl.BlockSpec(memory_space=pl.ANY)] * len(counts),
        scratch_shapes=[
            pltpu.SMEM((2, ranges.shape[0]), jnp.int32),
            pltpu.VMEM((1, rows), jnp.int32),
            pltpu.VMEM((1, HD // 2), jnp.float32),
            pltpu.VMEM((2 * vision, HD), jnp.bfloat16),
            pltpu.VMEM((rows, group), jnp.bfloat16),
            pltpu.VMEM(query.shape, jnp.bfloat16),
            pltpu.VMEM(key.shape, jnp.bfloat16),
            pltpu.VMEM(value.shape, jnp.bfloat16),
            pltpu.VMEM((packet, HD), jnp.bfloat16),
            pltpu.VMEM((2 * stacked, HD), jnp.bfloat16),
            pltpu.VMEM((2 * rows, HD), jnp.bfloat16),
            pltpu.SemaphoreType.DMA((9,)),
            pltpu.SemaphoreType.DMA((8,)),
        ],
        compiler_params=pltpu.CompilerParams(vmem_limit_bytes=60 * 2**20),
        name="prepare_first" if first else "prepare_second",
    )(
        jnp.transpose(ranges),
        positions.reshape(1, rows),
        frequency.reshape(1, HD // 2),
        vision_keys,
        vision_values,
        cross,
        query,
        key,
        value,
    )


def fold_keys(keys, values_turned, jobs, bounded=False):
    scale = HD**-0.5 * log2e
    spans = []
    for job in jobs:
        width = min(256, job[0].shape[0])
        for begin in range(0, job[0].shape[0], width):
            spans.append((job, slice(begin, begin + width)))
    scores = [
        lax.dot_general(
            keys, stacked_ref[span, :], contract_last, preferred_element_type=jnp.float32
        )
        for (stacked_ref, _, _, _), span in spans
    ]
    for ((_, peak_ref, total_ref, visible), span), score in zip(spans, scores):
        peak = peak_ref[0:1, span]
        seen = visible[:, span]
        if seen.shape[0] == 1:
            highest = 0.0 if bounded else jnp.max(score, axis=0, keepdims=True) * scale
            new_peak = jnp.where(seen, jnp.maximum(peak, highest), peak)
            weights = jnp.exp2(score * scale - jnp.where(seen, new_peak, -unseen))
        else:
            score = jnp.where(seen, score * scale, unseen)
            new_peak = jnp.maximum(peak, jnp.max(score, axis=0, keepdims=True))
            weights = jnp.where(seen, jnp.exp2(score - new_peak), 0.0)
        total_ref[:, span] = total_ref[:, span] * jnp.exp2(peak - new_peak) + jnp.dot(
            values_turned, weights.astype(jnp.bfloat16), preferred_element_type=jnp.float32
        )
        peak_ref[0:1, span] = new_peak


def clear(peak_ref, total_ref):
    peak_ref[...] = jnp.full(peak_ref.shape, unseen, jnp.float32)
    total_ref[...] = jnp.zeros(total_ref.shape, jnp.float32)


def finish_columns(peak_ref, total_ref):
    sums = total_ref[HD : HD + 1, :]
    some = sums > 0.0
    safe = jnp.where(some, sums, 1.0)
    log_sum = jnp.where(some, peak_ref[0:1, :] + jnp.log2(safe), unseen)
    return total_ref[:HD, :] / safe, log_sum


def turn_values(value, target_ref):
    target_ref[:HD, :] = value.T
    target_ref[HD:, :] = jnp.ones((stat_rows, target_ref.shape[1]), jnp.bfloat16)


def frame_numbers(inner):
    device = lax.axis_index("ctx")
    plane, place = device // inner, lax.rem(device, inner)
    near = plane + 1 - 2 * lax.rem(plane, 2)
    return (
        plane * inner + place,
        plane * inner + 1 - place,
        near * inner + place,
        near * inner + 1 - place,
    )


def cross_kernel(inner, heads, columns, places, units, chosen, resumed, finish, table_source, *refs):
    refs = list(refs)
    arrays = sorted({places[number][0] for number, frames in units if frames})
    arrays = {array: refs.pop(0) for array in arrays}
    query_refs = {}
    for number, frames in units:
        if frames:
            array, row = places[number]
            query_refs[number] = arrays[array].at[pl.ds(row, columns), :]
    frame_refs = [refs.pop(0) for _ in chosen]
    state_refs = [refs.pop(0) for _ in range(2)] if resumed else None
    out_refs, (turned_ref, peaks_ref, totals_ref, table_ref, semaphore) = refs[:-5], refs[-5:]
    load = pltpu.make_async_copy(table_source, table_ref, semaphore)
    load.start()
    if finish == "state":
        peaks_ref, totals_ref = out_refs
    lanes = heads * TBLOCK
    blocks = columns // lanes
    frames = frame_numbers(inner)
    vision = turned_ref.shape[2]
    for turn, (number, _) in enumerate(units):
        if resumed:
            peaks_ref[turn] = state_refs[0][number]
            totals_ref[turn] = state_refs[1][number]
        else:
            clear(peaks_ref.at[turn], totals_ref.at[turn])

    def job(turn, number, flags):
        visible = jnp.concatenate([jnp.full((1, lanes), flag, jnp.int32) for flag in flags], axis=1)
        return query_refs[number], peaks_ref.at[turn], totals_ref.at[turn], visible > 0

    for slot, index in enumerate(chosen):
        turn_values(frame_refs[slot][vision : 2 * vision, :], turned_ref.at[slot])
        if slot == 0:
            load.wait()
        keys = frame_refs[slot][:vision, :]
        limit = largest_square(keys)[0, 0] * (1.05 * (HD**-0.5 * log2e / score_limit) ** 2)
        members = []
        for turn, (number, indices) in enumerate(units):
            if index not in indices:
                continue
            flags = []
            for block in range(blocks):
                at = number * (2 * blocks + 1) + 2 * block
                inside = jnp.logical_and(
                    table_ref[at] <= frames[index], frames[index] < table_ref[at + 1]
                )
                flags.append(inside.astype(jnp.int32))
            needed = functools.reduce(jnp.maximum, flags)
            square = table_ref[number * (2 * blocks + 1) + 2 * blocks].astype(jnp.float32)
            bounded = (square * limit < 1.0).astype(jnp.int32)
            members.append((turn, number, flags, needed * bounded, needed * (1 - bounded)))

        def fold(taken, bounded):
            jobs = [job(turn, number, flags) for turn, number, flags, _, _ in taken]
            fold_keys(frame_refs[slot][:vision, :], turned_ref[slot], jobs, bounded)

        for begin in range(0, len(members), 2):
            pair = members[begin : begin + 2]
            count = sum(member[3] for member in pair)
            if len(pair) == 2:
                pl.when(count == 2)(functools.partial(fold, pair, True))
            for member in pair:
                alone = jnp.logical_and(count == 1, member[3] == 1)
                pl.when(alone)(functools.partial(fold, [member], True))
                pl.when(member[4] == 1)(functools.partial(fold, [member], False))

    if finish == "state":
        return
    stats = []
    for turn in range(len(units)):
        mixed, log_sum = finish_columns(peaks_ref.at[turn], totals_ref.at[turn])
        for block in range(blocks):
            span = slice(block * lanes, (block + 1) * lanes)
            stats.append(log_sum[:, span])
            row = (turn * blocks + block) * HD
            out_refs[0][row : row + HD, :] = mixed[:, span].astype(out_refs[0].dtype)
    stat = jnp.concatenate(stats, axis=0)
    if finish == "packed":
        high = stat.astype(jnp.bfloat16)
        rest = stat - high.astype(jnp.float32)
        middle = rest.astype(jnp.bfloat16)
        low = rest - middle.astype(jnp.float32)
        rows = [high.astype(jnp.float32), middle.astype(jnp.float32), low, jnp.zeros_like(stat)]
        out_refs[0][len(stats) * HD :, :] = jnp.concatenate(rows, axis=0).astype(jnp.bfloat16)
    else:
        out_refs[1][...] = stat


def cross_part(table, queries, frames, units, state, finish, rows, inner, heads):
    lanes = heads * TBLOCK
    columns = rows * heads
    vision = FRAME_LEN
    count = len(units) * (rows // TBLOCK)
    chosen = tuple(sorted({index for _, indices in units for index in indices}))
    if finish == "state":
        out_shape = (
            jax.ShapeDtypeStruct((len(units), 8, columns), jnp.float32),
            jax.ShapeDtypeStruct((len(units), HD + stat_rows, columns), jnp.float32),
        )
    elif finish == "packed":
        out_shape = (jax.ShapeDtypeStruct((count * HD + 4 * count, lanes), jnp.bfloat16),)
    else:
        out_shape = (
            jax.ShapeDtypeStruct((count * HD, lanes), jnp.float32),
            jax.ShapeDtypeStruct((count, lanes), jnp.float32),
        )
    packet = columns + 2 * rows + TBLOCK
    places = ((0, 0), (1, 0), (2, 0), (2, packet))
    arrays = sorted({places[number][0] for number, indices in units if indices})
    arguments = [queries[array] for array in arrays]
    arguments += [*(frames[index] for index in chosen), *state]
    return pl.pallas_call(
        functools.partial(
            cross_kernel, inner, heads, columns, places, units, chosen, len(state) > 0, finish
        ),
        out_shape=out_shape,
        in_specs=[pl.BlockSpec(memory_space=pl.ANY)] + whole(len(arguments)),
        out_specs=whole(len(out_shape)),
        scratch_shapes=[
            pltpu.VMEM((len(chosen), HD + stat_rows, vision), jnp.bfloat16),
            pltpu.VMEM((len(units), 8, columns), jnp.float32),
            pltpu.VMEM((len(units), HD + stat_rows, columns), jnp.float32),
            pltpu.SMEM(table.shape, jnp.int32),
            pltpu.SemaphoreType.DMA,
        ],
        compiler_params=pltpu.CompilerParams(vmem_limit_bytes=28 * 2**20),
        name="cross_" + finish,
    )(table, *arguments)


def self_kernel(inner, heads, rows, own_ref, beside_ref, *refs):
    key_value_refs, out_ref = refs[:6], refs[6]
    key_ref, value_ref, turned_ref, peak_ref, total_ref = refs[7:]
    device = lax.axis_index("ctx")
    plane, place = device // inner, lax.rem(device, inner)
    lanes = heads * TBLOCK
    columns = rows * heads
    vision = beside_ref.shape[0] - columns
    own_kv, partner_kv, near_kv, across_kv, far_kv, last_kv = key_value_refs
    packet = own_kv.shape[0]
    vision_rows = near_kv.shape[0] - 2 * rows
    tails = [(own_kv, columns), (partner_kv, columns), (near_kv, vision_rows)]
    tails += [(across_kv, vision_rows), (far_kv, columns), (far_kv, packet + columns)]
    tails += [(last_kv, 0), (last_kv, 2 * rows)]
    for slot, (ref, begin) in enumerate(tails):
        span = slice(slot * rows, (slot + 1) * rows)
        key_ref[span, :] = ref[begin : begin + rows, :]
        value_ref[span, :] = ref[begin + rows : begin + 2 * rows, :]
    turn_values(value_ref[...], turned_ref)
    planes = (plane, plane + 1 - 2 * lax.rem(plane, 2), lax.rem(plane + 2, 4), 3 - plane)
    starts = []
    for source in planes:
        starts.append((source * inner + place) * rows)
        starts.append((source * inner + 1 - place) * rows)
    down = lax.broadcasted_iota(jnp.int32, (rows, columns), 0)
    key_index = jnp.concatenate([down + start for start in starts], axis=0)
    across = lax.broadcasted_iota(jnp.int32, key_index.shape, 1)
    token = (across // lanes) * TBLOCK + lax.rem(across, TBLOCK)
    queries = (own_ref, beside_ref.at[pl.ds(vision, columns), :])
    for slot, query_ref in enumerate(queries):
        side = place if slot == 0 else 1 - place
        clear(peak_ref, total_ref)
        visible = key_index <= token + (plane * inner + side) * rows
        fold_keys(key_ref[...], turned_ref[...], [(query_ref, peak_ref, total_ref, visible)])
        mixed, _ = finish_columns(peak_ref, total_ref)
        for block in range(rows // TBLOCK):
            part = mixed[:, block * lanes : (block + 1) * lanes].T.astype(jnp.bfloat16)
            for head in range(heads):
                out_ref[block * inner + side, :, head * HD : (head + 1) * HD] = part[
                    head * TBLOCK : (head + 1) * TBLOCK
                ]


def self_part(own, beside, key_values, rows, inner, heads):
    return pl.pallas_call(
        functools.partial(self_kernel, inner, heads, rows),
        out_shape=jax.ShapeDtypeStruct((inner * rows // TBLOCK, TBLOCK, heads * HD), jnp.bfloat16),
        in_specs=whole(2 + len(key_values)),
        out_specs=whole(1)[0],
        scratch_shapes=[
            pltpu.VMEM((8 * rows, HD), jnp.bfloat16),
            pltpu.VMEM((8 * rows, HD), jnp.bfloat16),
            pltpu.VMEM((HD + stat_rows, 8 * rows), jnp.bfloat16),
            pltpu.VMEM((8, rows * heads), jnp.float32),
            pltpu.VMEM((HD + stat_rows, rows * heads), jnp.float32),
        ],
        compiler_params=pltpu.CompilerParams(vmem_limit_bytes=24 * 2**20),
        name="self_attention",
    )(own, beside, *key_values)


def combine_kernel(inner, heads, gate_ref, mixed_ref, stat_ref, returned_ref, out_ref):
    count = stat_ref.shape[0]
    side = count // inner
    place = lax.rem(lax.axis_index("ctx"), inner)
    gate = jnp.tanh(jnp.full((1, heads * TBLOCK), gate_ref[0], jnp.float32))
    stats = returned_ref[count * HD :, :].astype(jnp.float32)
    far_stat = stats[:count] + stats[count : 2 * count] + stats[2 * count : 3 * count]
    own_stat = stat_ref[...]
    peak = jnp.maximum(own_stat, far_stat)
    own_weight = jnp.exp2(own_stat - peak)
    far_weight = jnp.exp2(far_stat - peak)
    ratio = gate / (own_weight + far_weight)
    own_weight, far_weight = own_weight * ratio, far_weight * ratio
    for block in range(count):
        target = (block % side) * inner + (place if block < side else 1 - place)
        span = slice(block * HD, (block + 1) * HD)
        mixed = mixed_ref[span, :] * own_weight[block : block + 1] + returned_ref[span, :].astype(
            jnp.float32
        ) * far_weight[block : block + 1]
        part = mixed.T.astype(jnp.bfloat16)
        for head in range(heads):
            out_ref[target, :, head * HD : (head + 1) * HD] = part[
                head * TBLOCK : (head + 1) * TBLOCK
            ]


def combine(gate_scale, mixed, stat, returned, inner, heads):
    return pl.pallas_call(
        functools.partial(combine_kernel, inner, heads),
        out_shape=jax.ShapeDtypeStruct((stat.shape[0], TBLOCK, heads * HD), jnp.bfloat16),
        in_specs=[pl.BlockSpec(memory_space=pltpu.SMEM)] + whole(3),
        out_specs=whole(1)[0],
        compiler_params=pltpu.CompilerParams(vmem_limit_bytes=16 * 2**20),
        name="combine_planes",
    )(gate_scale, mixed, stat, returned)


def spread_kernel(in_ref, out_ref):
    group = in_ref.shape[2]
    for head in range(in_ref.shape[0]):
        out_ref[:, head * group : (head + 1) * group] = in_ref[head]


def spread(inward):
    count, rows, columns = inward.shape
    return pl.pallas_call(
        spread_kernel,
        out_shape=jax.ShapeDtypeStruct((rows, count * columns), inward.dtype),
        in_specs=whole(1),
        out_specs=whole(1)[0],
        compiler_params=pltpu.CompilerParams(vmem_limit_bytes=16 * 2**20),
        name="spread_heads",
    )(inward)


def on_device_split(
    axes,
    query_self,
    key_self,
    value_self,
    positions,
    query_cross,
    key_vision,
    value_vision,
    media_range,
    gate_scale,
):
    inner = key_self.shape[1] // HD
    heads = query_self.shape[1] // key_self.shape[1]
    rows = query_self.shape[0]
    group = heads * HD
    columns = axes["head"]
    devices = axes["ctx"]
    plane_count = devices // inner

    def place_of(device):
        return device // inner, device % inner

    def send(values, turn, flip, upward=0):
        pairs = []
        for device in range(devices):
            plane, place = place_of(device)
            target = plane ^ turn
            if upward == 0 or target ^ upward < target:
                pairs.append((device, target * inner + (place ^ flip)))
        return lax.ppermute(values, "ctx", pairs)

    exponents = np.arange(HD // 2) * (2.0 / HD)
    frequency = jnp.asarray(np.power(rope_base, -exponents), jnp.float32)
    sources = (positions, frequency, key_vision, value_vision, query_cross, query_self, key_self)
    near_out, other = prepare(media_range, *sources, value_self, inner, True)
    partner = send(other, 0, 1)
    near = send(near_out, 1, 0)
    value_self, near_out, other = lax.optimization_barrier((value_self, near_out, other))
    beside_out, own, own_self, across_out = prepare(media_range, *sources, value_self, inner, False)
    beside = send(beside_out, 0, 1)
    packets = jnp.concatenate([own, partner], axis=0)
    far = send(packets, 2, 0)
    across_out, partner = lax.optimization_barrier((across_out, partner))
    across = send(across_out, 1, 1)
    tail = slice(rows * heads, rows * heads + 2 * rows)
    last = send(jnp.concatenate([own[tail], partner[tail]], axis=0), 3, 0, upward=3)

    queries = (own, partner, far)
    count = own.shape[0]
    table = [values[count - TBLOCK, : 2 * (rows // TBLOCK) + 1] for values in queries]
    table.append(far[2 * count - TBLOCK, : 2 * (rows // TBLOCK) + 1])
    first_table = jnp.concatenate(table[:2]).astype(jnp.int32)
    table = jnp.concatenate(table).astype(jnp.int32)
    frames = (near_out, beside, near, across)
    sizes = (rows, inner, heads)
    units = ((0, (0, 2)), (1, (0, 2)), (2, ()), (3, ()))
    state = cross_part(first_table, queries, frames, units, (), "state", *sizes)
    units = ((0, ()), (1, ()), (2, (0, 2)), (3, (0, 2)))
    state = cross_part(table, queries, frames, units, state, "state", *sizes)
    units = ((0, (1,)), (1, (1,)), (2, (1,)), (3, (1,)))
    state = cross_part(table, queries, frames, units, state, "state", *sizes)
    units = ((2, (3,)), (3, (3,)))
    (outgoing,) = cross_part(table, queries, frames, units, state, "packed", *sizes)
    outgoing, last = lax.optimization_barrier((outgoing, last))
    returned = send(outgoing, 2, 0)
    outgoing, table, own_self = lax.optimization_barrier((outgoing, table, own_self))
    units = ((0, (3,)), (1, (3,)))
    mixed, stat = cross_part(table, queries, frames, units, state, "own", *sizes)
    self_rows = self_part(
        own_self, beside, (own, partner, near, across, far, last), *sizes
    )
    planes = [
        [
            (plane * inner + place) * columns + column
            for column in range(columns)
            for place in range(inner)
        ]
        for plane in range(plane_count)
    ]

    def exchange(outward):
        inward = lax.all_to_all(
            outward.reshape(-1, outward.shape[2]),
            ("ctx", "head"),
            0,
            0,
            axis_index_groups=planes,
            tiled=True,
        )
        return spread(inward.reshape(outward.shape))

    self_context = exchange(self_rows)
    cross_context = exchange(combine(gate_scale, mixed, stat, returned, inner, heads))
    return self_context, cross_context


def on_device(axes, *arguments):
    query_self, key_self, _, _, _, key_vision, _, media_range, _ = arguments
    inner = key_self.shape[1] // HD
    heads = query_self.shape[1] // key_self.shape[1]
    rows = query_self.shape[0]
    suited = (
        inner == 2
        and axes["ctx"] == 4 * inner
        and heads * TBLOCK == HD
        and key_vision.shape[0] == FRAME_LEN
        and rows == axes["head"] * TBLOCK
        and media_range.shape[0] * TBLOCK == rows
    )
    if suited:
        return on_device_split(axes, *arguments)
    return on_device_gathered(*arguments)


def solution(mesh):
    placed = (
        P("ctx", "head"),
        P("ctx", "head"),
        P("ctx", "head"),
        P("ctx"),
        P("ctx", "head"),
        P("ctx", "head"),
        P("ctx", "head"),
        P("ctx", None),
        P(),
    )
    return jax.shard_map(
        functools.partial(on_device, dict(mesh.shape)),
        mesh=mesh,
        in_specs=placed,
        out_specs=(P(("ctx", "head"), None), P(("ctx", "head"), None)),
        check_vma=False,
    )
```

profile of v0, /device:TPU:0, one launch (start us, length us, event | category | flops | bytes accessed | tf_op | source)
XLA Modules:
  0.0 64.9 jit_solution(8993458019218293182)
XLA Ops:
  0.6 2.2 %prepare_first.1 = (bf16[1920,128]{1,0:T(8,128)(2,1)}, bf16[656,128]{1,0:T(8,128)(2,1)}) custom-call(s32[2,4]{1,0:T(2,128)} %bitcast.10, s32[1,64]{1,0:T(1,128)} %bitcast.12, f32[1,64]{1,0:T(1,128)} %constant.4.frequency_ref, bf16[896,256]{1,0:T(8,128)(2,1)} %vision_key_ref.3, bf16[896,256]{1,0:T(8,128)(2,1)} %vision_value_ref.3, ...), custom_call_target="tpu_custom_call" | custom-call | tf_op jit(solution)/shard_map/prepare_first/pallas_call | solution.py:329
  2.8 3.0 %collective-permute-start = (bf16[656,128]{1,0:T(8,128)(2,1)}, bf16[656,128]{1,0:T(8,128)(2,1)S(1)}, u32[]{:S(2)}, u32[]{:S(2)}) collective-permute-start(bf16[656,128]{1,0:T(8,128)(2,1)} %get-tuple-element.25), channel_id=1, source_target_pairs={{0,4},{4,0},{8,12},{12,8},{16,20},{20,16},{24,28},{28,24},{1,5},{5... | collective-permute-start | bytes 503816 | tf_op jit(solution)/shard_map/ppermute | solution.py:701
  5.9 0.0 copy-start.2
  5.9 1.6 %collective-permute-start.4 = (bf16[1920,128]{1,0:T(8,128)(2,1)}, bf16[1920,128]{1,0:T(8,128)(2,1)S(1)}, u32[]{:S(2)}, u32[]{:S(2)}) collective-permute-start(bf16[1920,128]{1,0:T(8,128)(2,1)} %get-tuple-element.32.refs_2_.refs_1_), channel_id=1, source_target_pairs={{0,8},{4,12},{8,0},{12,4},{16,24},{20,28},{24,16},{28,20},{1,9},{5... | collective-permute-start | bytes 1474568 | tf_op jit(solution)/shard_map/ppermute | solution.py:701
  7.4 2.4 %prepare_second.1 = (bf16[2304,128]{1,0:T(8,128)(2,1)}, bf16[656,128]{1,0:T(8,128)(2,1)}, bf16[512,128]{1,0:T(8,128)(2,1)}, bf16[1920,128]{1,0:T(8,128)(2,1)}) custom-call(s32[2,4]{1,0:T(2,128)} %bitcast.11, s32[1,64]{1,0:T(1,128)} %bitcast.13, f32[1,64]{1,0:T(1,128)} %constant.4.frequency_ref, bf16[896,256]{1,0:T(8,128)(2,1)} %vision_key_ref.3, ...), custom_call_target="tpu_custom_call" | custom-call | tf_op jit(solution)/shard_map/prepare_second/pallas_call | solution.py:329
  9.8 0.6 collective-permute-start.3
  10.4 0.8 %slice.22 = bf16[128,128]{1,0:T(8,128)(2,1)S(1)} slice(bf16[656,128]{1,0:T(8,128)(2,1)} %get-tuple-element.27.refs_0_), slice={[512:640], [0:128]} | slice | bytes 65536 | tf_op jit(solution)/shard_map/slice | solution.py:717
  11.2 0.7 %slice_bitcast_fusion.3 = bf16[9]{0:T(256)(128)(2,1)S(1)} fusion(bf16[656,128]{1,0:T(8,128)(2,1)} %get-tuple-element.27.refs_0_), kind=kLoop, calls=%fused_computation.7 | loop fusion | bytes 36 | tf_op jit(solution)/shard_map/squeeze | solution.py:721
  11.9 0.0 collective-permute-done.refs_1_
  11.9 0.9 %pad_maximum_fusion = bf16[1312,128]{1,0:T(8,128)(2,1)S(1)} fusion(bf16[656,128]{1,0:T(8,128)(2,1)S(1)} %collective-permute-done.refs_1_, bf16[656,128]{1,0:T(8,128)(2,1)} %get-tuple-element.27.refs_0_), kind=kLoop, calls=%fused_computation | loop fusion | flops 671744 | bytes 671744 | tf_op jit(solution)/shard_map/concatenate | solution.py:712
  12.8 2.7 %collective-permute-start.1 = (bf16[1312,128]{1,0:T(8,128)(2,1)S(1)}, bf16[1312,128]{1,0:T(8,128)(2,1)S(1)}, u32[]{:S(2)}, u32[]{:S(2)}) collective-permute-start(bf16[1312,128]{1,0:T(8,128)(2,1)S(1)} %pad_maximum_fusion), channel_id=1, source_target_pairs={{0,16},{4,20},{8,24},{12,28},{16,0},{20,4},{24,8},{28,12},{1,17},{... | collective-permute-start | bytes 1007624 | tf_op jit(solution)/shard_map/ppermute | solution.py:701
  15.5 1.9 %collective-permute-start.2 = (bf16[1920,128]{1,0:T(8,128)(2,1)}, bf16[1920,128]{1,0:T(8,128)(2,1)S(1)}, u32[]{:S(2)}, u32[]{:S(2)}) collective-permute-start(bf16[1920,128]{1,0:T(8,128)(2,1)} %get-tuple-element.30), channel_id=1, source_target_pairs={{0,12},{4,8},{8,4},{12,0},{16,28},{20,24},{24,20},{28,16},{1,13},{... | collective-permute-start | bytes 1474568 | tf_op jit(solution)/shard_map/ppermute | solution.py:701
  17.4 2.8 %collective-permute-start.5 = (bf16[256,128]{1,0:T(8,128)(2,1)S(1)}, bf16[256,128]{1,0:T(8,128)(2,1)S(1)}, u32[]{:S(2)}, u32[]{:S(2)}) collective-permute-start(bf16[256,128]{1,0:T(8,128)(2,1)S(1)} %pad_maximum_fusion.1), channel_id=1, source_target_pairs={{0,24},{4,28},{8,16},{12,20},{1,25},{5,29},{9,17},{13,21},{2,26},{... | collective-permute-start | bytes 196616 | tf_op jit(solution)/shard_map/ppermute | solution.py:701
  20.1 0.1 maximum_convert_fusion.1.table_source
  20.2 5.5 %collective-permute-done.4.refs_3_.refs_2_ = bf16[1920,128]{1,0:T(8,128)(2,1)S(1)} collective-permute-done((bf16[1920,128]{1,0:T(8,128)(2,1)}, bf16[1920,128]{1,0:T(8,128)(2,1)S(1)}, u32[]{:S(2)}, u32[]{:S(2)}) %collective-permute-start.4) | collective-permute-done | bytes 491552 | tf_op jit(solution)/shard_map/ppermute | solution.py:701
  25.7 0.0 copy-done.2
  25.7 0.0 copy-start
  25.7 0.9 %copy-done = bf16[656,128]{1,0:T(8,128)(2,1)S(1)} copy-done((bf16[656,128]{1,0:T(8,128)(2,1)S(1)}, bf16[656,128]{1,0:T(8,128)(2,1)}, u32[]{:S(2)}) %copy-start) | copy-done | bytes 167960
  26.6 2.3 %cross_state.3 = (f32[4,8,512]{2,1,0:T(8,128)S(1)}, f32[4,144,512]{2,1,0:T(8,128)S(1)}) custom-call(s32[18]{0:T(128)S(1)} %maximum_convert_fusion.1.table_source, bf16[656,128]{1,0:T(8,128)(2,1)S(1)} %copy-done, bf16[656,128]{1,0:T(8,128)(2,1)S(1)} %collective-permute-done.refs_1_, bf16[1920,128]{1,0:T(8,128)(2,1)S(1)} %copy-done.2, ...), custom_call_target="tpu_custom_call" | custom-call | tf_op jit(solution)/shard_map/cross_state/pallas_call | solution.py:536
  28.9 1.0 %collective-permute-done.1.refs_0_.refs_2_.refs_4_ = bf16[1312,128]{1,0:T(8,128)(2,1)S(1)} collective-permute-done((bf16[1312,128]{1,0:T(8,128)(2,1)S(1)}, bf16[1312,128]{1,0:T(8,128)(2,1)S(1)}, u32[]{:S(2)}, u32[]{:S(2)}) %collective-permute-start.1) | collective-permute-done | bytes 335904 | tf_op jit(solution)/shard_map/ppermute | solution.py:701
  29.9 0.1 maximum_convert_fusion.table_source
  30.0 0.0 copy-start.1
  30.0 5.6 %cross_state.4 = (f32[4,8,512]{2,1,0:T(8,128)S(1)}, f32[4,144,512]{2,1,0:T(8,128)S(1)}) custom-call(s32[36]{0:T(128)S(1)} %maximum_convert_fusion.table_source, bf16[1312,128]{1,0:T(8,128)(2,1)S(1)} %collective-permute-done.1.refs_0_.refs_2_.refs_4_, bf16[1920,128]{1,0:T(8,128)(2,1)S(1)} %copy-done.2, ...), custom_call_target="tpu_custom_call" | custom-call | tf_op jit(solution)/shard_map/cross_state/pallas_call | solution.py:536
  35.6 0.0 collective-permute-done.3.refs_3_.beside_ref
  35.6 0.0 copy-done.1
  35.6 3.0 %cross_state.5 = (f32[4,8,512]{2,1,0:T(8,128)S(1)}, f32[4,144,512]{2,1,0:T(8,128)S(1)}) custom-call(s32[36]{0:T(128)S(1)} %maximum_convert_fusion.table_source, bf16[656,128]{1,0:T(8,128)(2,1)S(1)} %copy-done.1, bf16[656,128]{1,0:T(8,128)(2,1)S(1)} %collective-permute-done.refs_1_, bf16[1312,128]{1,0:T(8,128)(2,1)S(1)} %collective-permute-done.1.refs_0_.refs_2_.refs_4_, ...), custom_call_target="tpu_custom_call" | custom-call | tf_op jit(solution)/shard_map/cross_state/pallas_call | solution.py:536
  38.6 0.0 copy-start.3
  38.6 0.0 collective-permute-done.2.refs_1_.refs_3_.refs_2_
  38.6 3.2 %cross_packed.1 = bf16[1056,128]{1,0:T(8,128)(2,1)S(1)} custom-call(s32[36]{0:T(128)S(1)} %maximum_convert_fusion.table_source, bf16[1312,128]{1,0:T(8,128)(2,1)S(1)} %collective-permute-done.1.refs_0_.refs_2_.refs_4_, bf16[1920,128]{1,0:T(8,128)(2,1)S(1)} %collective-permute-done.2.refs_1_.refs_3_.refs_2_, ...), custom_call_target="tpu_custom_call" | custom-call | tf_op jit(solution)/shard_map/cross_packed/pallas_call | solution.py:536
  41.9 0.0 collective-permute-done.5.refs_5_
  41.9 0.1 collective-permute-start.6
  42.0 0.0 copy-done.3
  42.0 2.0 %self_attention.1 = bf16[8,16,1024]{2,1,0:T(8,128)(2,1)} custom-call(bf16[512,128]{1,0:T(8,128)(2,1)S(1)} %copy-done.3, bf16[2304,128]{1,0:T(8,128)(2,1)S(1)} %collective-permute-done.3.refs_3_.beside_ref, bf16[656,128]{1,0:T(8,128)(2,1)S(1)} %copy-done.1, bf16[656,128]{1,0:T(8,128)(2,1)S(1)} %collective-permute-done.refs_1_, ...), custom_call_target="tpu_custom_call" | custom-call | tf_op jit(solution)/shard_map/self_attention/pallas_call | solution.py:599
  44.0 4.8 %all-to-all-start = ((bf16[8,16,1024]{2,1,0:T(8,128)(2,1)}), bf16[8,16,1024]{2,1,0:T(8,128)(2,1)S(1)}, u32[]{:S(2)}, u32[]{:S(2)}) async-start(bf16[8,16,1024]{2,1,0:T(8,128)(2,1)} %self_attention.1), calls=%async_computation | async-start | bytes 524288 | tf_op jit(solution)/shard_map/all_to_all | solution.py:753
  49.4 0.9 %cross_own.1 = (f32[1024,128]{1,0:T(8,128)S(1)}, f32[8,128]{1,0:T(8,128)S(1)}) custom-call(s32[36]{0:T(128)S(1)} %maximum_convert_fusion.table_source, bf16[656,128]{1,0:T(8,128)(2,1)S(1)} %copy-done.1, bf16[656,128]{1,0:T(8,128)(2,1)S(1)} %collective-permute-done.refs_1_, bf16[1920,128]{1,0:T(8,128)(2,1)S(1)} %collective-permute-done.2.refs_1_.refs_3_.refs_2_, ...), custom_call_target="tpu_custom_call" | custom-call | tf_op jit(solution)/shard_map/cross_own/pallas_call | solution.py:536
  50.3 3.1 %collective-permute-done.6.returned_ref = bf16[1056,128]{1,0:T(8,128)(2,1)S(1)} collective-permute-done((bf16[1056,128]{1,0:T(8,128)(2,1)S(1)}, bf16[1056,128]{1,0:T(8,128)(2,1)S(1)}, u32[]{:S(2)}, u32[]{:S(2)}) %collective-permute-start.6) | collective-permute-done | bytes 270368 | tf_op jit(solution)/shard_map/ppermute | solution.py:701
  53.5 0.9 %combine_planes.1 = bf16[8,16,1024]{2,1,0:T(8,128)(2,1)} custom-call(f32[1]{0:T(128)S(6)} %copy.12.gate_ref, f32[1024,128]{1,0:T(8,128)S(1)} %get-tuple-element.44.mixed_ref, f32[8,128]{1,0:T(8,128)S(1)} %get-tuple-element.45.stat_ref, bf16[1056,128]{1,0:T(8,128)(2,1)S(1)} %collective-permute-done.6.returned_ref), custom_call_target="tpu_custom_call" | custom-call | tf_op jit(solution)/shard_map/combine_planes/pallas_call | solution.py:643
  54.4 0.4 all-to-all-done.in_ref
  54.8 3.4 %all-to-all-start.1 = ((bf16[8,16,1024]{2,1,0:T(8,128)(2,1)}), bf16[8,16,1024]{2,1,0:T(8,128)(2,1)S(1)}, u32[]{:S(2)}, u32[]{:S(2)}) async-start(bf16[8,16,1024]{2,1,0:T(8,128)(2,1)} %combine_planes.1), calls=%async_computation.1 | async-start | bytes 524288 | tf_op jit(solution)/shard_map/all_to_all | solution.py:753
  58.2 0.7 %spread_heads.2 = bf16[16,8192]{1,0:T(8,128)(2,1)} custom-call(bf16[8,16,1024]{2,1,0:T(8,128)(2,1)S(1)} %all-to-all-done.in_ref), custom_call_target="tpu_custom_call" | custom-call | tf_op jit(solution)/shard_map/spread_heads/pallas_call | solution.py:661
  58.9 5.2 %all-to-all-done.1.in_ref = bf16[8,16,1024]{2,1,0:T(8,128)(2,1)S(1)} async-done(((bf16[8,16,1024]{2,1,0:T(8,128)(2,1)}), bf16[8,16,1024]{2,1,0:T(8,128)(2,1)S(1)}, u32[]{:S(2)}, u32[]{:S(2)}) %all-to-all-start.1) | async-done | bytes 262176 | tf_op jit(solution)/shard_map/all_to_all | solution.py:753
  64.2 0.7 %spread_heads.3 = bf16[16,8192]{1,0:T(8,128)(2,1)} custom-call(bf16[8,16,1024]{2,1,0:T(8,128)(2,1)S(1)} %all-to-all-done.1.in_ref), custom_call_target="tpu_custom_call" | custom-call | tf_op jit(solution)/shard_map/spread_heads/pallas_call | solution.py:661
  (4 shorter events, 0.0 us)
Async XLA Ops:
  2.8 9.0 %collective-permute-start = (bf16[656,128]{1,0:T(8,128)(2,1)}, bf16[656,128]{1,0:T(8,128)(2,1)S(1)}, u32[]{:S(2)}, u32[]{:S(2)}) collective-permute-start(bf16[656,128]{1,0:T(8,128)(2,1)} %get-tuple-element.25), channel_id=1, source_target_pairs={{0,4},{4,0},{8,12},{12,8},{16,20},{20,16},{24,28},{28,24},{1,5},{5... | collective-permute-start | bytes 503816 | tf_op jit(solution)/shard_map/ppermute | solution.py:701
  5.9 19.8 %copy-start.2 = (bf16[1920,128]{1,0:T(8,128)(2,1)S(1)}, bf16[1920,128]{1,0:T(8,128)(2,1)}, u32[]{:S(2)}) copy-start(bf16[1920,128]{1,0:T(8,128)(2,1)} %get-tuple-element.32.refs_2_.refs_1_) | copy-start | bytes 1474564
  5.9 19.8 %collective-permute-start.4 = (bf16[1920,128]{1,0:T(8,128)(2,1)}, bf16[1920,128]{1,0:T(8,128)(2,1)S(1)}, u32[]{:S(2)}, u32[]{:S(2)}) collective-permute-start(bf16[1920,128]{1,0:T(8,128)(2,1)} %get-tuple-element.32.refs_2_.refs_1_), channel_id=1, source_target_pairs={{0,8},{4,12},{8,0},{12,4},{16,24},{20,28},{24,16},{28,20},{1,9},{5... | collective-permute-start | bytes 1474568 | tf_op jit(solution)/shard_map/ppermute | solution.py:701
  9.8 25.7 %collective-permute-start.3 = (bf16[2304,128]{1,0:T(8,128)(2,1)}, bf16[2304,128]{1,0:T(8,128)(2,1)S(1)}, u32[]{:S(2)}, u32[]{:S(2)}) collective-permute-start(bf16[2304,128]{1,0:T(8,128)(2,1)} %get-tuple-element.31), channel_id=1, source_target_pairs={{0,4},{4,0},{8,12},{12,8},{16,20},{20,16},{24,28},{28,24},{1,5},{5... | collective-permute-start | bytes 1769480 | tf_op jit(solution)/shard_map/ppermute | solution.py:701
  12.8 17.1 %collective-permute-start.1 = (bf16[1312,128]{1,0:T(8,128)(2,1)S(1)}, bf16[1312,128]{1,0:T(8,128)(2,1)S(1)}, u32[]{:S(2)}, u32[]{:S(2)}) collective-permute-start(bf16[1312,128]{1,0:T(8,128)(2,1)S(1)} %pad_maximum_fusion), channel_id=1, source_target_pairs={{0,16},{4,20},{8,24},{12,28},{16,0},{20,4},{24,8},{28,12},{1,17},{... | collective-permute-start | bytes 1007624 | tf_op jit(solution)/shard_map/ppermute | solution.py:701
  15.5 23.1 %collective-permute-start.2 = (bf16[1920,128]{1,0:T(8,128)(2,1)}, bf16[1920,128]{1,0:T(8,128)(2,1)S(1)}, u32[]{:S(2)}, u32[]{:S(2)}) collective-permute-start(bf16[1920,128]{1,0:T(8,128)(2,1)} %get-tuple-element.30), channel_id=1, source_target_pairs={{0,12},{4,8},{8,4},{12,0},{16,28},{20,24},{24,20},{28,16},{1,13},{... | collective-permute-start | bytes 1474568 | tf_op jit(solution)/shard_map/ppermute | solution.py:701
  17.4 24.5 %collective-permute-start.5 = (bf16[256,128]{1,0:T(8,128)(2,1)S(1)}, bf16[256,128]{1,0:T(8,128)(2,1)S(1)}, u32[]{:S(2)}, u32[]{:S(2)}) collective-permute-start(bf16[256,128]{1,0:T(8,128)(2,1)S(1)} %pad_maximum_fusion.1), channel_id=1, source_target_pairs={{0,24},{4,28},{8,16},{12,20},{1,25},{5,29},{9,17},{13,21},{2,26},{... | collective-permute-start | bytes 196616 | tf_op jit(solution)/shard_map/ppermute | solution.py:701
  25.7 0.9 %copy-start = (bf16[656,128]{1,0:T(8,128)(2,1)S(1)}, bf16[656,128]{1,0:T(8,128)(2,1)}, u32[]{:S(2)}) copy-start(bf16[656,128]{1,0:T(8,128)(2,1)} %get-tuple-element.27.refs_0_) | copy-start | bytes 503812
  30.0 5.6 %copy-start.1 = (bf16[656,128]{1,0:T(8,128)(2,1)S(1)}, bf16[656,128]{1,0:T(8,128)(2,1)}, u32[]{:S(2)}) copy-start(bf16[656,128]{1,0:T(8,128)(2,1)} %get-tuple-element.27.refs_0_) | copy-start | bytes 503812
  38.6 3.4 %copy-start.3 = (bf16[512,128]{1,0:T(8,128)(2,1)S(1)}, bf16[512,128]{1,0:T(8,128)(2,1)}, u32[]{:S(2)}) copy-start(bf16[512,128]{1,0:T(8,128)(2,1)} %get-tuple-element.41.own_ref) | copy-start | bytes 393220
  41.9 11.6 %collective-permute-start.6 = (bf16[1056,128]{1,0:T(8,128)(2,1)S(1)}, bf16[1056,128]{1,0:T(8,128)(2,1)S(1)}, u32[]{:S(2)}, u32[]{:S(2)}) collective-permute-start(bf16[1056,128]{1,0:T(8,128)(2,1)S(1)} %cross_packed.1), channel_id=1, source_target_pairs={{0,16},{4,20},{8,24},{12,28},{16,0},{20,4},{24,8},{28,12},{1,17},{... | collective-permute-start | bytes 811016 | tf_op jit(solution)/shard_map/ppermute | solution.py:701
  44.0 10.8 %all-to-all-start = ((bf16[8,16,1024]{2,1,0:T(8,128)(2,1)}), bf16[8,16,1024]{2,1,0:T(8,128)(2,1)S(1)}, u32[]{:S(2)}, u32[]{:S(2)}) async-start(bf16[8,16,1024]{2,1,0:T(8,128)(2,1)} %self_attention.1), calls=%async_computation | async-start | bytes 524288 | tf_op jit(solution)/shard_map/all_to_all | solution.py:753
  54.8 9.4 %all-to-all-start.1 = ((bf16[8,16,1024]{2,1,0:T(8,128)(2,1)}), bf16[8,16,1024]{2,1,0:T(8,128)(2,1)S(1)}, u32[]{:S(2)}, u32[]{:S(2)}) async-start(bf16[8,16,1024]{2,1,0:T(8,128)(2,1)} %combine_planes.1), calls=%async_computation.1 | async-start | bytes 524288 | tf_op jit(solution)/shard_map/all_to_all | solution.py:753
where the time goes:
time: 65.4 us; the launch traced here: 64.9 us
  Pallas kernels  24 us (37%)
  starting transfers between devices  20.7 us (32%)
  waiting for transfers between devices  15.3 us (23%)
  local copies, waits for them, and re-layouts  2.38 us (4%)
  between operations  1.43 us (2%)
  other arithmetic  1.1 us (2%)
    pallas_call x5, Pallas kernels, cross_part(): pl.pallas_call(functools.partial(cross_kernel, inner, heads, columns, pla...  15 us
    ppermute x7, starting transfers between devices, send(): return lax.ppermute(values, 'ctx', pairs)  12.6 us
    ppermute x7, waiting for transfers between devices, send(): return lax.ppermute(values, 'ctx', pairs)  9.65 us
    all_to_all x2, starting transfers between devices, exchange(): lax.all_to_all(outward.reshape(-1, outward.shape[2]), ('ctx', 'head'), 0,...  8.16 us
    all_to_all x2, waiting for transfers between devices, exchange(): lax.all_to_all(outward.reshape(-1, outward.shape[2]), ('ctx', 'head'), 0,...  5.65 us
    pallas_call x2, Pallas kernels, prepare(): pl.pallas_call(functools.partial(prepare_kernel, inner, first), out_shape...  4.59 us
    pallas_call x1, Pallas kernels, self_part(): pl.pallas_call(functools.partial(self_kernel, inner, heads, rows), out_sh...  2.02 us
    pallas_call x2, Pallas kernels, spread(): pl.pallas_call(spread_kernel, out_shape=jax.ShapeDtypeStruct((rows, count...  1.44 us
  transfers between devices with their start and end apart: 9, of which 5 were waited for; matrix products, arithmetic and copies ran while one was open for 4% of the time, Pallas kernels for 32%

commit v1 on v0

--- a/solution.py
+++ b/solution.py
@@ -372,10 +372,11 @@
         lax.dot_general(
             keys, stacked_ref[span, :], contract_last, preferred_element_type=jnp.float32
         )
-        for (stacked_ref, _, _, _), span in spans
+        for (stacked_ref, *_), span in spans
     ]
-    for ((_, peak_ref, total_ref, visible), span), score in zip(spans, scores):
-        peak = peak_ref[0:1, span]
+    for (job, span), score in zip(spans, scores):
+        _, peak_ref, total_ref, visible, old_peak_ref, old_total_ref = job
+        peak = old_peak_ref[0:1, span]
         seen = visible[:, span]
         if seen.shape[0] == 1:
             highest = 0.0 if bounded else jnp.max(score, axis=0, keepdims=True) * scale
@@ -385,7 +386,7 @@
             score = jnp.where(seen, score * scale, unseen)
             new_peak = jnp.maximum(peak, jnp.max(score, axis=0, keepdims=True))
             weights = jnp.where(seen, jnp.exp2(score - new_peak), 0.0)
-        total_ref[:, span] = total_ref[:, span] * jnp.exp2(peak - new_peak) + jnp.dot(
+        total_ref[:, span] = old_total_ref[:, span] * jnp.exp2(peak - new_peak) + jnp.dot(
             values_turned, weights.astype(jnp.bfloat16), preferred_element_type=jnp.float32
         )
         peak_ref[0:1, span] = new_peak
@@ -441,16 +442,23 @@
     blocks = columns // lanes
     frames = frame_numbers(inner)
     vision = turned_ref.shape[2]
+
+    def resume(turn, number):
+        peaks_ref[turn] = state_refs[0][number]
+        totals_ref[turn] = state_refs[1][number]
+
     for turn, (number, _) in enumerate(units):
-        if resumed:
-            peaks_ref[turn] = state_refs[0][number]
-            totals_ref[turn] = state_refs[1][number]
-        else:
+        if resumed and not units[turn][1]:
+            resume(turn, number)
+        elif not resumed:
             clear(peaks_ref.at[turn], totals_ref.at[turn])
 
-    def job(turn, number, flags):
+    def job(turn, number, flags, index):
         visible = jnp.concatenate([jnp.full((1, lanes), flag, jnp.int32) for flag in flags], axis=1)
-        return query_refs[number], peaks_ref.at[turn], totals_ref.at[turn], visible > 0
+        here = (peaks_ref.at[turn], totals_ref.at[turn])
+        begins = resumed and index == units[turn][1][0]
+        before = (state_refs[0].at[number], state_refs[1].at[number]) if begins else here
+        return query_refs[number], *here, visible > 0, *before
 
     for slot, index in enumerate(chosen):
         turn_values(frame_refs[slot][vision : 2 * vision, :], turned_ref.at[slot])
@@ -470,12 +478,14 @@
                 )
                 flags.append(inside.astype(jnp.int32))
             needed = functools.reduce(jnp.maximum, flags)
+            if resumed and index == indices[0]:
+                pl.when(needed == 0)(functools.partial(resume, turn, number))
             square = table_ref[number * (2 * blocks + 1) + 2 * blocks].astype(jnp.float32)
             bounded = (square * limit < 1.0).astype(jnp.int32)
             members.append((turn, number, flags, needed * bounded, needed * (1 - bounded)))
 
         def fold(taken, bounded):
-            jobs = [job(turn, number, flags) for turn, number, flags, _, _ in taken]
+            jobs = [job(turn, number, flags, index) for turn, number, flags, _, _ in taken]
             fold_keys(frame_refs[slot][:vision, :], turned_ref[slot], jobs, bounded)
 
         for begin in range(0, len(members), 2):
@@ -585,7 +595,7 @@
         side = place if slot == 0 else 1 - place
         clear(peak_ref, total_ref)
         visible = key_index <= token + (plane * inner + side) * rows
-        fold_keys(key_ref[...], turned_ref[...], [(query_ref, peak_ref, total_ref, visible)])
+        fold_keys(key_ref[...], turned_ref[...], [(query_ref, peak_ref, total_ref, visible, peak_ref, total_ref)])
         mixed, _ = finish_columns(peak_ref, total_ref)
         for block in range(rows // TBLOCK):
             part = mixed[:, block * lanes : (block + 1) * lanes].T.astype(jnp.bfloat16)

time: 65.4 us -> 66.3 us (1.014)
  no operation moved by 1% of the time
where the time goes in v1:
time: 66.3 us; the launch traced here: 65.2 us
  Pallas kernels  24.1 us (36%)
  starting transfers between devices  20.9 us (32%)
  waiting for transfers between devices  15.3 us (23%)
  local copies, waits for them, and re-layouts  2.38 us (4%)
  between operations  1.42 us (2%)
  other arithmetic  1.1 us (2%)
    pallas_call x5, Pallas kernels, cross_part(): pl.pallas_call(functools.partial(cross_kernel, inner, heads, columns, pla...  15.2 us
    ppermute x7, starting transfers between devices, send(): return lax.ppermute(values, 'ctx', pairs)  12.6 us
    ppermute x7, waiting for transfers between devices, send(): return lax.ppermute(values, 'ctx', pairs)  9.76 us
    all_to_all x2, starting transfers between devices, exchange(): lax.all_to_all(outward.reshape(-1, outward.shape[2]), ('ctx', 'head'), 0,...  8.34 us
    all_to_all x2, waiting for transfers between devices, exchange(): lax.all_to_all(outward.reshape(-1, outward.shape[2]), ('ctx', 'head'), 0,...  5.58 us
    pallas_call x2, Pallas kernels, prepare(): pl.pallas_call(functools.partial(prepare_kernel, inner, first), out_shape...  4.59 us
    pallas_call x1, Pallas kernels, self_part(): pl.pallas_call(functools.partial(self_kernel, inner, heads, rows), out_sh...  2.02 us
    pallas_call x2, Pallas kernels, spread(): pl.pallas_call(spread_kernel, out_shape=jax.ShapeDtypeStruct((rows, count...  1.44 us
  transfers between devices with their start and end apart: 9, of which 5 were waited for; matrix products, arithmetic and copies ran while one was open for 4% of the time, Pallas kernels for 32%

profile of v1, /device:TPU:0, one launch (start us, length us, event | category | flops | bytes accessed | tf_op | source)
XLA Modules:
  0.0 65.2 jit_solution(7137335214518890806)
XLA Ops:
  0.6 2.2 %prepare_first.1 = (bf16[1920,128]{1,0:T(8,128)(2,1)}, bf16[656,128]{1,0:T(8,128)(2,1)}) custom-call(s32[2,4]{1,0:T(2,128)} %bitcast.10, s32[1,64]{1,0:T(1,128)} %bitcast.12, f32[1,64]{1,0:T(1,128)} %constant.4.frequency_ref, bf16[896,256]{1,0:T(8,128)(2,1)} %vision_key_ref.3, bf16[896,256]{1,0:T(8,128)(2,1)} %vision_value_ref.3, ...), custom_call_target="tpu_custom_call" | custom-call | tf_op jit(solution)/shard_map/prepare_first/pallas_call | solution.py:329
  2.8 3.0 %collective-permute-start = (bf16[656,128]{1,0:T(8,128)(2,1)}, bf16[656,128]{1,0:T(8,128)(2,1)S(1)}, u32[]{:S(2)}, u32[]{:S(2)}) collective-permute-start(bf16[656,128]{1,0:T(8,128)(2,1)} %get-tuple-element.25), channel_id=1, source_target_pairs={{0,4},{4,0},{8,12},{12,8},{16,20},{20,16},{24,28},{28,24},{1,5},{5... | collective-permute-start | bytes 503816 | tf_op jit(solution)/shard_map/ppermute | solution.py:711
  5.9 0.0 copy-start.2
  5.9 1.6 %collective-permute-start.4 = (bf16[1920,128]{1,0:T(8,128)(2,1)}, bf16[1920,128]{1,0:T(8,128)(2,1)S(1)}, u32[]{:S(2)}, u32[]{:S(2)}) collective-permute-start(bf16[1920,128]{1,0:T(8,128)(2,1)} %get-tuple-element.32.refs_2_.refs_1_), channel_id=1, source_target_pairs={{0,8},{4,12},{8,0},{12,4},{16,24},{20,28},{24,16},{28,20},{1,9},{5... | collective-permute-start | bytes 1474568 | tf_op jit(solution)/shard_map/ppermute | solution.py:711
  7.4 2.4 %prepare_second.1 = (bf16[2304,128]{1,0:T(8,128)(2,1)}, bf16[656,128]{1,0:T(8,128)(2,1)}, bf16[512,128]{1,0:T(8,128)(2,1)}, bf16[1920,128]{1,0:T(8,128)(2,1)}) custom-call(s32[2,4]{1,0:T(2,128)} %bitcast.11, s32[1,64]{1,0:T(1,128)} %bitcast.13, f32[1,64]{1,0:T(1,128)} %constant.4.frequency_ref, bf16[896,256]{1,0:T(8,128)(2,1)} %vision_key_ref.3, ...), custom_call_target="tpu_custom_call" | custom-call | tf_op jit(solution)/shard_map/prepare_second/pallas_call | solution.py:329
  9.8 0.6 collective-permute-start.3
  10.4 0.8 %slice.22 = bf16[128,128]{1,0:T(8,128)(2,1)S(1)} slice(bf16[656,128]{1,0:T(8,128)(2,1)} %get-tuple-element.27.refs_0_), slice={[512:640], [0:128]} | slice | bytes 65536 | tf_op jit(solution)/shard_map/slice | solution.py:727
  11.2 0.7 %slice_bitcast_fusion.3 = bf16[9]{0:T(256)(128)(2,1)S(1)} fusion(bf16[656,128]{1,0:T(8,128)(2,1)} %get-tuple-element.27.refs_0_), kind=kLoop, calls=%fused_computation.7 | loop fusion | bytes 36 | tf_op jit(solution)/shard_map/squeeze | solution.py:731
  11.9 0.0 collective-permute-done.refs_1_
  11.9 0.9 %pad_maximum_fusion = bf16[1312,128]{1,0:T(8,128)(2,1)S(1)} fusion(bf16[656,128]{1,0:T(8,128)(2,1)S(1)} %collective-permute-done.refs_1_, bf16[656,128]{1,0:T(8,128)(2,1)} %get-tuple-element.27.refs_0_), kind=kLoop, calls=%fused_computation | loop fusion | flops 671744 | bytes 671744 | tf_op jit(solution)/shard_map/concatenate | solution.py:722
  12.8 2.7 %collective-permute-start.1 = (bf16[1312,128]{1,0:T(8,128)(2,1)S(1)}, bf16[1312,128]{1,0:T(8,128)(2,1)S(1)}, u32[]{:S(2)}, u32[]{:S(2)}) collective-permute-start(bf16[1312,128]{1,0:T(8,128)(2,1)S(1)} %pad_maximum_fusion), channel_id=1, source_target_pairs={{0,16},{4,20},{8,24},{12,28},{16,0},{20,4},{24,8},{28,12},{1,17},{... | collective-permute-start | bytes 1007624 | tf_op jit(solution)/shard_map/ppermute | solution.py:711
  15.5 1.9 %collective-permute-start.2 = (bf16[1920,128]{1,0:T(8,128)(2,1)}, bf16[1920,128]{1,0:T(8,128)(2,1)S(1)}, u32[]{:S(2)}, u32[]{:S(2)}) collective-permute-start(bf16[1920,128]{1,0:T(8,128)(2,1)} %get-tuple-element.30), channel_id=1, source_target_pairs={{0,12},{4,8},{8,4},{12,0},{16,28},{20,24},{24,20},{28,16},{1,13},{... | collective-permute-start | bytes 1474568 | tf_op jit(solution)/shard_map/ppermute | solution.py:711
  17.4 2.8 %collective-permute-start.5 = (bf16[256,128]{1,0:T(8,128)(2,1)S(1)}, bf16[256,128]{1,0:T(8,128)(2,1)S(1)}, u32[]{:S(2)}, u32[]{:S(2)}) collective-permute-start(bf16[256,128]{1,0:T(8,128)(2,1)S(1)} %pad_maximum_fusion.1), channel_id=1, source_target_pairs={{0,24},{4,28},{8,16},{12,20},{1,25},{5,29},{9,17},{13,21},{2,26},{... | collective-permute-start | bytes 196616 | tf_op jit(solution)/shard_map/ppermute | solution.py:711
  20.1 0.1 maximum_convert_fusion.1.table_source
  20.2 5.5 %collective-permute-done.4.refs_3_.refs_2_ = bf16[1920,128]{1,0:T(8,128)(2,1)S(1)} collective-permute-done((bf16[1920,128]{1,0:T(8,128)(2,1)}, bf16[1920,128]{1,0:T(8,128)(2,1)S(1)}, u32[]{:S(2)}, u32[]{:S(2)}) %collective-permute-start.4) | collective-permute-done | bytes 491552 | tf_op jit(solution)/shard_map/ppermute | solution.py:711
  25.7 0.0 copy-done.2
  25.7 0.0 copy-start
  25.7 0.9 %copy-done = bf16[656,128]{1,0:T(8,128)(2,1)S(1)} copy-done((bf16[656,128]{1,0:T(8,128)(2,1)S(1)}, bf16[656,128]{1,0:T(8,128)(2,1)}, u32[]{:S(2)}) %copy-start) | copy-done | bytes 167960
  26.6 2.3 %cross_state.3 = (f32[4,8,512]{2,1,0:T(8,128)S(1)}, f32[4,144,512]{2,1,0:T(8,128)S(1)}) custom-call(s32[18]{0:T(128)S(1)} %maximum_convert_fusion.1.table_source, bf16[656,128]{1,0:T(8,128)(2,1)S(1)} %copy-done, bf16[656,128]{1,0:T(8,128)(2,1)S(1)} %collective-permute-done.refs_1_, bf16[1920,128]{1,0:T(8,128)(2,1)S(1)} %copy-done.2, ...), custom_call_target="tpu_custom_call" | custom-call | tf_op jit(solution)/shard_map/cross_state/pallas_call | solution.py:546
  28.9 1.0 %collective-permute-done.1.refs_0_.refs_2_.refs_4_ = bf16[1312,128]{1,0:T(8,128)(2,1)S(1)} collective-permute-done((bf16[1312,128]{1,0:T(8,128)(2,1)S(1)}, bf16[1312,128]{1,0:T(8,128)(2,1)S(1)}, u32[]{:S(2)}, u32[]{:S(2)}) %collective-permute-start.1) | collective-permute-done | bytes 335904 | tf_op jit(solution)/shard_map/ppermute | solution.py:711
  29.9 0.1 maximum_convert_fusion.table_source
  30.0 0.0 copy-start.1
  30.0 5.6 %cross_state.4 = (f32[4,8,512]{2,1,0:T(8,128)S(1)}, f32[4,144,512]{2,1,0:T(8,128)S(1)}) custom-call(s32[36]{0:T(128)S(1)} %maximum_convert_fusion.table_source, bf16[1312,128]{1,0:T(8,128)(2,1)S(1)} %collective-permute-done.1.refs_0_.refs_2_.refs_4_, bf16[1920,128]{1,0:T(8,128)(2,1)S(1)} %copy-done.2, ...), custom_call_target="tpu_custom_call" | custom-call | tf_op jit(solution)/shard_map/cross_state/pallas_call | solution.py:546
  35.6 0.0 collective-permute-done.3.refs_3_.beside_ref
  35.6 0.0 copy-done.1
  35.6 3.1 %cross_state.5 = (f32[4,8,512]{2,1,0:T(8,128)S(1)}, f32[4,144,512]{2,1,0:T(8,128)S(1)}) custom-call(s32[36]{0:T(128)S(1)} %maximum_convert_fusion.table_source, bf16[656,128]{1,0:T(8,128)(2,1)S(1)} %copy-done.1, bf16[656,128]{1,0:T(8,128)(2,1)S(1)} %collective-permute-done.refs_1_, bf16[1312,128]{1,0:T(8,128)(2,1)S(1)} %collective-permute-done.1.refs_0_.refs_2_.refs_4_, ...), custom_call_target="tpu_custom_call" | custom-call | tf_op jit(solution)/shard_map/cross_state/pallas_call | solution.py:546
  38.7 0.0 copy-start.3
  38.7 0.0 collective-permute-done.2.refs_1_.refs_3_.refs_2_
  38.7 3.3 %cross_packed.1 = bf16[1056,128]{1,0:T(8,128)(2,1)S(1)} custom-call(s32[36]{0:T(128)S(1)} %maximum_convert_fusion.table_source, bf16[1312,128]{1,0:T(8,128)(2,1)S(1)} %collective-permute-done.1.refs_0_.refs_2_.refs_4_, bf16[1920,128]{1,0:T(8,128)(2,1)S(1)} %collective-permute-done.2.refs_1_.refs_3_.refs_2_, ...), custom_call_target="tpu_custom_call" | custom-call | tf_op jit(solution)/shard_map/cross_packed/pallas_call | solution.py:546
  42.0 0.0 collective-permute-done.5.refs_5_
  42.0 0.1 collective-permute-start.6
  42.1 0.0 copy-done.3
  42.1 2.0 %self_attention.1 = bf16[8,16,1024]{2,1,0:T(8,128)(2,1)} custom-call(bf16[512,128]{1,0:T(8,128)(2,1)S(1)} %copy-done.3, bf16[2304,128]{1,0:T(8,128)(2,1)S(1)} %collective-permute-done.3.refs_3_.beside_ref, bf16[656,128]{1,0:T(8,128)(2,1)S(1)} %copy-done.1, bf16[656,128]{1,0:T(8,128)(2,1)S(1)} %collective-permute-done.refs_1_, ...), custom_call_target="tpu_custom_call" | custom-call | tf_op jit(solution)/shard_map/self_attention/pallas_call | solution.py:609
  44.1 4.8 %all-to-all-start = ((bf16[8,16,1024]{2,1,0:T(8,128)(2,1)}), bf16[8,16,1024]{2,1,0:T(8,128)(2,1)S(1)}, u32[]{:S(2)}, u32[]{:S(2)}) async-start(bf16[8,16,1024]{2,1,0:T(8,128)(2,1)} %self_attention.1), calls=%async_computation | async-start | bytes 524288 | tf_op jit(solution)/shard_map/all_to_all | solution.py:763
  49.5 1.0 %cross_own.1 = (f32[1024,128]{1,0:T(8,128)S(1)}, f32[8,128]{1,0:T(8,128)S(1)}) custom-call(s32[36]{0:T(128)S(1)} %maximum_convert_fusion.table_source, bf16[656,128]{1,0:T(8,128)(2,1)S(1)} %copy-done.1, bf16[656,128]{1,0:T(8,128)(2,1)S(1)} %collective-permute-done.refs_1_, bf16[1920,128]{1,0:T(8,128)(2,1)S(1)} %collective-permute-done.2.refs_1_.refs_3_.refs_2_, ...), custom_call_target="tpu_custom_call" | custom-call | tf_op jit(solution)/shard_map/cross_own/pallas_call | solution.py:546
  50.5 3.3 %collective-permute-done.6.returned_ref = bf16[1056,128]{1,0:T(8,128)(2,1)S(1)} collective-permute-done((bf16[1056,128]{1,0:T(8,128)(2,1)S(1)}, bf16[1056,128]{1,0:T(8,128)(2,1)S(1)}, u32[]{:S(2)}, u32[]{:S(2)}) %collective-permute-start.6) | collective-permute-done | bytes 270368 | tf_op jit(solution)/shard_map/ppermute | solution.py:711
  53.8 0.9 %combine_planes.1 = bf16[8,16,1024]{2,1,0:T(8,128)(2,1)} custom-call(f32[1]{0:T(128)S(6)} %copy.12.gate_ref, f32[1024,128]{1,0:T(8,128)S(1)} %get-tuple-element.44.mixed_ref, f32[8,128]{1,0:T(8,128)S(1)} %get-tuple-element.45.stat_ref, bf16[1056,128]{1,0:T(8,128)(2,1)S(1)} %collective-permute-done.6.returned_ref), custom_call_target="tpu_custom_call" | custom-call | tf_op jit(solution)/shard_map/combine_planes/pallas_call | solution.py:653
  54.6 0.3 all-to-all-done.in_ref
  54.9 3.6 %all-to-all-start.1 = ((bf16[8,16,1024]{2,1,0:T(8,128)(2,1)}), bf16[8,16,1024]{2,1,0:T(8,128)(2,1)S(1)}, u32[]{:S(2)}, u32[]{:S(2)}) async-start(bf16[8,16,1024]{2,1,0:T(8,128)(2,1)} %combine_planes.1), calls=%async_computation.1 | async-start | bytes 524288 | tf_op jit(solution)/shard_map/all_to_all | solution.py:763
  58.5 0.7 %spread_heads.2 = bf16[16,8192]{1,0:T(8,128)(2,1)} custom-call(bf16[8,16,1024]{2,1,0:T(8,128)(2,1)S(1)} %all-to-all-done.in_ref), custom_call_target="tpu_custom_call" | custom-call | tf_op jit(solution)/shard_map/spread_heads/pallas_call | solution.py:671
  59.2 5.3 %all-to-all-done.1.in_ref = bf16[8,16,1024]{2,1,0:T(8,128)(2,1)S(1)} async-done(((bf16[8,16,1024]{2,1,0:T(8,128)(2,1)}), bf16[8,16,1024]{2,1,0:T(8,128)(2,1)S(1)}, u32[]{:S(2)}, u32[]{:S(2)}) %all-to-all-start.1) | async-done | bytes 262176 | tf_op jit(solution)/shard_map/all_to_all | solution.py:763
  64.5 0.7 %spread_heads.3 = bf16[16,8192]{1,0:T(8,128)(2,1)} custom-call(bf16[8,16,1024]{2,1,0:T(8,128)(2,1)S(1)} %all-to-all-done.1.in_ref), custom_call_target="tpu_custom_call" | custom-call | tf_op jit(solution)/shard_map/spread_heads/pallas_call | solution.py:671
  (4 shorter events, 0.0 us)
Async XLA Ops:
  2.8 9.0 %collective-permute-start = (bf16[656,128]{1,0:T(8,128)(2,1)}, bf16[656,128]{1,0:T(8,128)(2,1)S(1)}, u32[]{:S(2)}, u32[]{:S(2)}) collective-permute-start(bf16[656,128]{1,0:T(8,128)(2,1)} %get-tuple-element.25), channel_id=1, source_target_pairs={{0,4},{4,0},{8,12},{12,8},{16,20},{20,16},{24,28},{28,24},{1,5},{5... | collective-permute-start | bytes 503816 | tf_op jit(solution)/shard_map/ppermute | solution.py:711
  5.9 19.8 %copy-start.2 = (bf16[1920,128]{1,0:T(8,128)(2,1)S(1)}, bf16[1920,128]{1,0:T(8,128)(2,1)}, u32[]{:S(2)}) copy-start(bf16[1920,128]{1,0:T(8,128)(2,1)} %get-tuple-element.32.refs_2_.refs_1_) | copy-start | bytes 1474564
  5.9 19.8 %collective-permute-start.4 = (bf16[1920,128]{1,0:T(8,128)(2,1)}, bf16[1920,128]{1,0:T(8,128)(2,1)S(1)}, u32[]{:S(2)}, u32[]{:S(2)}) collective-permute-start(bf16[1920,128]{1,0:T(8,128)(2,1)} %get-tuple-element.32.refs_2_.refs_1_), channel_id=1, source_target_pairs={{0,8},{4,12},{8,0},{12,4},{16,24},{20,28},{24,16},{28,20},{1,9},{5... | collective-permute-start | bytes 1474568 | tf_op jit(solution)/shard_map/ppermute | solution.py:711
  9.8 25.7 %collective-permute-start.3 = (bf16[2304,128]{1,0:T(8,128)(2,1)}, bf16[2304,128]{1,0:T(8,128)(2,1)S(1)}, u32[]{:S(2)}, u32[]{:S(2)}) collective-permute-start(bf16[2304,128]{1,0:T(8,128)(2,1)} %get-tuple-element.31), channel_id=1, source_target_pairs={{0,4},{4,0},{8,12},{12,8},{16,20},{20,16},{24,28},{28,24},{1,5},{5... | collective-permute-start | bytes 1769480 | tf_op jit(solution)/shard_map/ppermute | solution.py:711
  12.8 17.1 %collective-permute-start.1 = (bf16[1312,128]{1,0:T(8,128)(2,1)S(1)}, bf16[1312,128]{1,0:T(8,128)(2,1)S(1)}, u32[]{:S(2)}, u32[]{:S(2)}) collective-permute-start(bf16[1312,128]{1,0:T(8,128)(2,1)S(1)} %pad_maximum_fusion), channel_id=1, source_target_pairs={{0,16},{4,20},{8,24},{12,28},{16,0},{20,4},{24,8},{28,12},{1,17},{... | collective-permute-start | bytes 1007624 | tf_op jit(solution)/shard_map/ppermute | solution.py:711
  15.5 23.2 %collective-permute-start.2 = (bf16[1920,128]{1,0:T(8,128)(2,1)}, bf16[1920,128]{1,0:T(8,128)(2,1)S(1)}, u32[]{:S(2)}, u32[]{:S(2)}) collective-permute-start(bf16[1920,128]{1,0:T(8,128)(2,1)} %get-tuple-element.30), channel_id=1, source_target_pairs={{0,12},{4,8},{8,4},{12,0},{16,28},{20,24},{24,20},{28,16},{1,13},{... | collective-permute-start | bytes 1474568 | tf_op jit(solution)/shard_map/ppermute | solution.py:711
  17.4 24.6 %collective-permute-start.5 = (bf16[256,128]{1,0:T(8,128)(2,1)S(1)}, bf16[256,128]{1,0:T(8,128)(2,1)S(1)}, u32[]{:S(2)}, u32[]{:S(2)}) collective-permute-start(bf16[256,128]{1,0:T(8,128)(2,1)S(1)} %pad_maximum_fusion.1), channel_id=1, source_target_pairs={{0,24},{4,28},{8,16},{12,20},{1,25},{5,29},{9,17},{13,21},{2,26},{... | collective-permute-start | bytes 196616 | tf_op jit(solution)/shard_map/ppermute | solution.py:711
  25.7 0.9 %copy-start = (bf16[656,128]{1,0:T(8,128)(2,1)S(1)}, bf16[656,128]{1,0:T(8,128)(2,1)}, u32[]{:S(2)}) copy-start(bf16[656,128]{1,0:T(8,128)(2,1)} %get-tuple-element.27.refs_0_) | copy-start | bytes 503812
  30.0 5.6 %copy-start.1 = (bf16[656,128]{1,0:T(8,128)(2,1)S(1)}, bf16[656,128]{1,0:T(8,128)(2,1)}, u32[]{:S(2)}) copy-start(bf16[656,128]{1,0:T(8,128)(2,1)} %get-tuple-element.27.refs_0_) | copy-start | bytes 503812
  38.7 3.4 %copy-start.3 = (bf16[512,128]{1,0:T(8,128)(2,1)S(1)}, bf16[512,128]{1,0:T(8,128)(2,1)}, u32[]{:S(2)}) copy-start(bf16[512,128]{1,0:T(8,128)(2,1)} %get-tuple-element.41.own_ref) | copy-start | bytes 393220
  42.0 11.8 %collective-permute-start.6 = (bf16[1056,128]{1,0:T(8,128)(2,1)S(1)}, bf16[1056,128]{1,0:T(8,128)(2,1)S(1)}, u32[]{:S(2)}, u32[]{:S(2)}) collective-permute-start(bf16[1056,128]{1,0:T(8,128)(2,1)S(1)} %cross_packed.1), channel_id=1, source_target_pairs={{0,16},{4,20},{8,24},{12,28},{16,0},{20,4},{24,8},{28,12},{1,17},{... | collective-permute-start | bytes 811016 | tf_op jit(solution)/shard_map/ppermute | solution.py:711
  44.1 10.8 %all-to-all-start = ((bf16[8,16,1024]{2,1,0:T(8,128)(2,1)}), bf16[8,16,1024]{2,1,0:T(8,128)(2,1)S(1)}, u32[]{:S(2)}, u32[]{:S(2)}) async-start(bf16[8,16,1024]{2,1,0:T(8,128)(2,1)} %self_attention.1), calls=%async_computation | async-start | bytes 524288 | tf_op jit(solution)/shard_map/all_to_all | solution.py:763
  54.9 9.6 %all-to-all-start.1 = ((bf16[8,16,1024]{2,1,0:T(8,128)(2,1)}), bf16[8,16,1024]{2,1,0:T(8,128)(2,1)S(1)}, u32[]{:S(2)}, u32[]{:S(2)}) async-start(bf16[8,16,1024]{2,1,0:T(8,128)(2,1)} %combine_planes.1), calls=%async_computation.1 | async-start | bytes 524288 | tf_op jit(solution)/shard_map/all_to_all | solution.py:763
